TPU v7x, 256 devices: a whole 4x4x8 slice. The times are simulated.
256 devices in a mesh: dp: 8 (over y, core), tm: 32 (over z, x).
Axes of the slice: x: 4, y: 4, z: 8, core: 2. Of those that a mesh axis runs over, the one named last changes fastest.
Arguments:
- frames: bfloat16 [65536, 1536], P(('dp', 'tm')), may hold values from -28 to 28, as said below
- seg: int32 [8, 8192], P('dp'), may hold values from 0 to 3, never falling along the last dimension, each value on 1 to 4096 neighbouring positions
- look_back: int32 [8, 32], P('dp'), may hold values 0 or 1
- w_dw: float32 [5, 1536], replicated, may hold values from -2.5 to 2.5
- w_qkv: bfloat16 [1536, 4608], P(None, 'dp'), may hold values from -0.15625 to 0.15625
- w_o: bfloat16 [1536, 1536], replicated, may hold values from -1.5 to 1.5
- cotangent: bfloat16 [65536, 1536], P(('dp', 'tm')), may hold values from -1 to 1
Outputs:
- mixed: bfloat16 [65536, 1536], P(('dp', 'tm'))
- weight_grad: float32 [1536, 1536], P('tm', 'dp')
Inputs may be any that keep to these rules, and one draw needn't show every extreme that they name: Float features; a few short runs of frames may be several times larger than the rest. `seg`: recording numbers never fall along a replica's frames; each recording has 1 to 4096 frames, one exactly 4096.
All inputs are finite; a program needn't handle non-finite values. No bound on the sum of `look_back` on one device may be relied on, other than what follows from the above.
Results may differ from a plain program's by a relative error of at most 0.012.
The roundings to bfloat16 on the way count: a program that leaves them out, or rounds other values in their place, can miss the bound.
Values may be sent and summed in bfloat16 or wider, within the bound.
A program may use at most 128 MiB of HBM per device.

v0:
```python
import math
import jax
import jax.numpy as jnp
from jax import lax
from jax.sharding import PartitionSpec as P

KER = 5
HEADS = 16
HALF = KER // 2


def conv_silu(rows_in, seg_in, w_dw):
    count = rows_in.shape[0] - 2 * HALF
    own = seg_in[HALF : HALF + count]
    total = jnp.zeros((count, rows_in.shape[1]), jnp.float32)
    for offset in range(KER):
        same = (seg_in[offset : offset + count] == own).astype(jnp.float32)
        total = (
            total
            + w_dw[offset] * rows_in[offset : offset + count].astype(jnp.float32) * same[:, None]
        )
    return jax.nn.silu(total).astype(jnp.bfloat16)


def local(frames, seg, look_back, w_dw, w_qkv, w_o, cotangent):
    rows, width = frames.shape
    count = lax.axis_size("tm")
    me = lax.axis_index("tm")
    weights = lax.all_gather(w_qkv, "dp", axis=1, tiled=True)
    before = lax.ppermute(frames, "tm", [(i, i + 1) for i in range(count - 1)])
    far = lax.ppermute(frames[-HALF:], "tm", [(i, i + 2) for i in range(count - 2)])
    after = lax.ppermute(frames[:HALF], "tm", [(i + 1, i) for i in range(count - 1)])
    stack = jnp.concatenate([far, before, frames, after], 0)
    seg_padded = jnp.pad(seg[0], (rows + HALF, HALF), constant_values=-1)
    local_seg = lax.dynamic_slice_in_dim(seg_padded, me * rows, 2 * rows + 2 * HALF, 0)
    activ = conv_silu(stack, local_seg, w_dw)
    qkv = jnp.dot(activ[rows:], weights, preferred_element_type=jnp.float32).astype(jnp.bfloat16)
    kv_before = jnp.dot(
        activ[:rows], weights[:, width:], preferred_element_type=jnp.float32
    ).astype(jnp.bfloat16)
    head_dim = width // HEADS
    queries = qkv[:, :width].reshape(rows, HEADS, head_dim)
    kv = jnp.concatenate([kv_before, qkv[:, width:]], 0).reshape(2 * rows, 2, HEADS, head_dim)
    scores = jnp.einsum("qhd,khd->hqk", queries, kv[:, 0], preferred_element_type=jnp.float32) * (
        1.0 / math.sqrt(head_dim)
    )
    seg_pair = local_seg[HALF : HALF + 2 * rows]
    same_rec = seg_pair[rows:][:, None] == seg_pair[None, :]
    look = lax.dynamic_slice_in_dim(look_back[0], me, 1, 0)[0] == 1
    allowed = same_rec & ((jnp.arange(2 * rows) >= rows) | look)[None, :]
    scores = jnp.where(allowed[None], scores, -1e30)
    raw = jnp.exp(scores - jnp.max(scores, axis=-1, keepdims=True))
    probs = (raw / jnp.sum(raw, axis=-1, keepdims=True)).astype(jnp.bfloat16)
    attn = jnp.einsum("hqk,khv->qhv", probs, kv[:, 1], preferred_element_type=jnp.float32)
    attn = attn.astype(jnp.bfloat16).reshape(rows, width)
    mixed = jnp.dot(attn, w_o, preferred_element_type=jnp.float32).astype(jnp.bfloat16)
    grad_term = lax.dot_general(
        attn, cotangent, (((0,), (0,)), ((), ())), preferred_element_type=jnp.float32
    )
    col_share = lax.psum_scatter(grad_term, "dp", scatter_dimension=1, tiled=True)
    weight_grad = lax.psum_scatter(col_share, "tm", scatter_dimension=0, tiled=True)
    return (mixed, weight_grad)


def solution(mesh):
    placed = (
        P(("dp", "tm"), None),
        P("dp", None),
        P("dp", None),
        P(),
        P(None, "dp"),
        P(),
        P(("dp", "tm"), None),
    )
    return jax.shard_map(
        local,
        mesh=mesh,
        in_specs=placed,
        out_specs=(P(("dp", "tm"), None), P("tm", "dp")),
        check_vma=False,
    )
```

profile of v0, /device:TPU:8, one launch (start us, length us, event | category | flops | bytes accessed | tf_op | source)
XLA Modules:
  0.0 419.2 jit_solution(788652810859067581)
XLA Ops:
  7.2 0.7 all-gather.2.cloned.1.call-update
  8.0 3.4 collective-permute-start.1
  11.4 0.8 fusion.22
  12.2 4.6 %collective-permute-start = (bf16[2,1536]{1,0:T(2,128)(2,1)S(1)}, bf16[2,1536]{1,0:T(2,128)(2,1)S(1)}, u32[]{:S(2)}, u32[]{:S(2)}) collective-permute-start(bf16[2,1536]{1,0:T(2,128)(2,1)S(1)} %get-tuple-element.13), channel_id=1, source_target_pairs={{0,2},{1,3},{2,4},{3,5},{4,6},{5,7},{6,8},{7,9},{8,10},{9,11},{10,... | collective-permute-start | bytes 18440 | tf_op jit(solution)/shard_map/ppermute | solution.py:31
  16.8 1.3 collective-permute-start.2
  18.1 0.8 pad_dynamic-slice_fusion
  18.9 0.1 slice.102
  19.0 0.1 slice.85
  19.1 1.2 fusion.23
  20.3 0.7 fusion.19
  20.9 1.1 slice_reduce_fusion.4
  22.1 0.1 fusion.15
  22.1 0.2 compare_and_fusion
  22.3 6.2 %collective-permute-done.1 = bf16[256,1536]{1,0:T(8,128)(2,1)S(1)} collective-permute-done((bf16[256,1536]{1,0:T(8,128)(2,1)}, bf16[256,1536]{1,0:T(8,128)(2,1)S(1)}, u32[]{:S(2)}, u32[]{:S(2)}) %collective-permute-start.1) | collective-permute-done | bytes 786464 | tf_op jit(solution)/shard_map/ppermute | solution.py:30
  28.7 0.4 pad_maximum_fusion.1
  29.1 5.4 %multiply_convert_fusion = bf16[512,1536]{1,0:T(8,128)(2,1)} fusion(bf16[514,1536]{1,0:T(8,128)(2,1)S(1)} %constant_dynamic-update-slice_fusion, bf16[514,1536]{1,0:T(8,128)(2,1)S(1)} %pad_maximum_fusion.1, bf16[256,1536]{1,0:T(8,128)(2,1)S(1)} %copy-done.1, bf16[256,1536]{1,0:T(8,128)(2,1)S(1)} %collective-permute-done.1, f32[512]{0:T(512)S(1)} %get-tuple-element.16, ...), kind=kLoop, calls=%fused_computation.14 | loop fusion | flops 20447232 | bytes 9476096 | tf_op jit(solution)/shard_map/convert_element_type | solution.py:22
  34.5 54.3 %all-gather.2.cloned.1.call-done = bf16[1536,4608]{0,1:T(8,128)(2,1)} async-done(((bf16[1536,576]{0,1:T(8,128)(2,1)}), bf16[1536,4608]{0,1:T(8,128)(2,1)}) %all-gather.2.cloned.1.call-update) | async-done | bytes 14155792 | tf_op jit(solution)/shard_map/all_gather | solution.py:29
  88.8 9.1 %convolution_convert_fusion = bf16[256,4608]{1,0:T(8,128)(2,1)S(1)} fusion(bf16[1536,4608]{0,1:T(8,128)(2,1)} %all-gather.2.cloned.1.call-done, bf16[512,1536]{1,0:T(8,128)(2,1)} %multiply_convert_fusion), kind=kOutput, calls=%fused_computation.6 | convolution fusion | flops 3625058304 | bytes 17301504 | tf_op jit(solution)/shard_map/dot_general | solution.py:37
  97.9 0.2 slice.112
  98.1 2.0 copy-done.4
  100.2 6.4 %fusion.8 = bf16[256,3072]{1,0:T(8,128)(2,1)S(1)} fusion(bf16[1536,4608]{0,1:T(8,128)(2,1)} %all-gather.2.cloned.1.call-done, bf16[512,1536]{1,0:T(8,128)(2,1)S(1)} %copy-done.4), kind=kOutput, calls=%fused_computation.12 | convolution fusion | flops 2416705536 | bytes 11796480 | tf_op jit(solution)/shard_map/dot_general | solution.py:38
  106.6 1.9 pad_maximum_fusion
  108.5 4.8 %copy.16 = bf16[512,3072]{0,1:T(8,128)(2,1)} copy(bf16[512,3072]{1,0:T(8,128)(2,1)} %pad_maximum_fusion) | data formatting | bytes 6291456 | tf_op jit(solution)/shard_map/concatenate | solution.py:43
  113.2 0.3 copy.17
  113.5 2.7 fusion.11
  116.2 6.0 %fusion.24 = (f32[16,256]{1,0:T(8,128)S(1)}, f32[16,256,512]{2,1,0:T(8,128)}) fusion(f32[16,256,512]{2,1,0:T(8,128)S(1)} %fusion.11, pred[256,512]{1,0:T(8,128)(4,1)S(1)} %compare_and_fusion), kind=kOutput, calls=%fused_computation.48 | output fusion | flops 12583423 | bytes 16924672 | tf_op jit(solution)/shard_map/sub | solution.py:52
  122.3 4.9 %fusion.12 = bf16[16,96,256]{2,1,0:T(8,128)(2,1)S(1)} fusion(f32[16,256,512]{2,1,0:T(8,128)} %get-tuple-element.20, f32[16,256]{1,0:T(8,128)S(1)} %get-tuple-element.19, bf16[512,2,16,96]{0,3,2,1:T(8,128)(2,1)S(1)} %bitcast.23), kind=kOutput, calls=%fused_computation.20 | convolution fusion | flops 407240704 | bytes 10764288 | tf_op jit(solution)/shard_map/hqk,khv->qhv/dot_general | solution.py:54
  127.2 5.1 %fusion.25 = f32[1536,1536]{0,1:T(8,128)} fusion(bf16[256,1536]{0,1:T(8,128)(2,1)S(1)} %bitcast.25, bf16[256,1536]{1,0:T(8,128)(2,1)S(1)} %copy-done), kind=kOutput, calls=%fused_computation.49 | convolution fusion | flops 1207959552 | bytes 11010048 | tf_op jit(solution)/shard_map/dot_general | solution.py:57
  132.3 58.7 %reduce-scatter.5.cloned.1.call-done = f32[1536,192]{0,1:T(8,128)} async-done(((f32[1536,1536]{0,1:T(8,128)}), f32[1536,192]{0,1:T(8,128)}) %reduce-scatter.5.cloned.1.call-update) | async-done | bytes 1179664 | tf_op jit(solution)/shard_map/reduce_scatter | solution.py:60
  191.0 2.9 copy.19
  193.9 4.6 %convolution_convert_fusion.1 = bf16[256,1536]{1,0:T(8,128)(2,1)} fusion(bf16[256,1536]{0,1:T(8,128)(2,1)S(1)} %bitcast.26, bf16[1536,1536]{1,0:T(8,128)(2,1)} %param.12), kind=kOutput, calls=%fused_computation.15 | convolution fusion | flops 1208352768 | bytes 6291456 | tf_op jit(solution)/shard_map/dot_general | solution.py:56
  198.5 214.1 %reduce-scatter.7.cloned.1.call-done = f32[48,192]{1,0:T(8,128)} async-done(((f32[1536,192]{1,0:T(8,128)}), f32[48,192]{1,0:T(8,128)}) %reduce-scatter.7.cloned.1.call-update) | async-done | bytes 36880
  (21 shorter events, 0.3 us)
Async XLA Ops:
  7.2 120.0 %copy-start = (bf16[256,1536]{1,0:T(8,128)(2,1)S(1)}, bf16[256,1536]{1,0:T(8,128)(2,1)}, u32[]{:S(2)}) copy-start(bf16[256,1536]{1,0:T(8,128)(2,1)} %param.13) | copy-start | bytes 2359300
  7.2 21.4 %copy-start.1 = (bf16[256,1536]{1,0:T(8,128)(2,1)S(1)}, bf16[256,1536]{1,0:T(8,128)(2,1)}, u32[]{:S(2)}) copy-start(bf16[256,1536]{1,0:T(8,128)(2,1)} %param.7) | copy-start | bytes 2359300
  7.2 81.6 %all-gather.2.cloned.1.call-start = ((), (), s32[]{:S(2)}) async-start(), calls=%async_computation.2 | async-start | bytes 15925248 | tf_op jit(solution)/shard_map/all_gather | solution.py:29
  7.9 183.1 %reduce-scatter.5.cloned.1.call-start = ((), (), s32[]{:S(2)}) async-start(), calls=%async_computation.3 | async-start | bytes 10616832 | tf_op jit(solution)/shard_map/reduce_scatter | solution.py:60
  8.0 20.6 %collective-permute-start.1 = (bf16[256,1536]{1,0:T(8,128)(2,1)}, bf16[256,1536]{1,0:T(8,128)(2,1)S(1)}, u32[]{:S(2)}, u32[]{:S(2)}) collective-permute-start(bf16[256,1536]{1,0:T(8,128)(2,1)} %param.7), channel_id=1, source_target_pairs={{0,1},{1,2},{2,3},{3,4},{4,5},{5,6},{6,7},{7,8},{8,9},{9,10},{10,1... | collective-permute-start | bytes 2359304 | tf_op jit(solution)/shard_map/ppermute | solution.py:30
  12.2 16.5 %collective-permute-start = (bf16[2,1536]{1,0:T(2,128)(2,1)S(1)}, bf16[2,1536]{1,0:T(2,128)(2,1)S(1)}, u32[]{:S(2)}, u32[]{:S(2)}) collective-permute-start(bf16[2,1536]{1,0:T(2,128)(2,1)S(1)} %get-tuple-element.13), channel_id=1, source_target_pairs={{0,2},{1,3},{2,4},{3,5},{4,6},{5,7},{6,8},{7,9},{8,10},{9,11},{10,... | collective-permute-start | bytes 18440 | tf_op jit(solution)/shard_map/ppermute | solution.py:31
  16.8 11.8 %collective-permute-start.2 = (bf16[2,1536]{1,0:T(2,128)(2,1)S(1)}, bf16[2,1536]{1,0:T(2,128)(2,1)S(1)}, u32[]{:S(2)}, u32[]{:S(2)}) collective-permute-start(bf16[2,1536]{1,0:T(2,128)(2,1)S(1)} %get-tuple-element.14), channel_id=1, source_target_pairs={{1,0},{2,1},{3,2},{4,3},{5,4},{6,5},{7,6},{8,7},{9,8},{10,9},{11,1... | collective-permute-start | bytes 18440 | tf_op jit(solution)/shard_map/ppermute | solution.py:32
  97.9 8.7 %copy-start.3 = (bf16[256,4608]{1,0:T(8,128)(2,1)}, bf16[256,4608]{1,0:T(8,128)(2,1)S(1)}, u32[]{:S(2)}) copy-start(bf16[256,4608]{1,0:T(8,128)(2,1)S(1)} %convolution_convert_fusion) | copy-start | bytes 7077892
  97.9 2.3 copy-start.4
  108.5 4.8 %slice-start = ((bf16[256,4608]{1,0:T(8,128)(2,1)}), bf16[256,1536]{1,0:T(8,128)(2,1)S(1)}, s32[]{:S(2)}) async-start(bf16[256,4608]{1,0:T(8,128)(2,1)} %copy-done.3), calls=%async_computation.5 | async-start | bytes 1572864 | tf_op jit(solution)/shard_map/slice | solution.py:42
  116.2 6.0 %copy-start.2 = (bf16[512,3072]{0,1:T(8,128)(2,1)S(1)}, bf16[512,3072]{0,1:T(8,128)(2,1)}, u32[]{:S(2)}) copy-start(bf16[512,3072]{0,1:T(8,128)(2,1)} %copy.16) | copy-start | bytes 9437188
  132.3 280.4 %reduce-scatter.7.cloned.1.call-start = ((), (), s32[]{:S(2)}) async-start(), calls=%async_computation.4 | async-start | bytes 1622016
Sparse Core Ops, SparseCore 0:
  9.9 78.8 all-gather.1
  132.4 58.5 reduce-scatter.4
  195.4 217.2 reduce-scatter.6
where the time goes:
time: 420 us; the launch traced here: 419 us
  waiting for transfers between devices  334 us (80%)
  matrix products  32.8 us (8%)
  other arithmetic  15.8 us (4%)
  between operations  13.9 us (3%)
  local copies, waits for them, and re-layouts  13.1 us (3%)
  starting transfers between devices  9.47 us (2%)
    unnamed x4, waiting for transfers between devices  215 us
    reduce_scatter x1, waiting for transfers between devices, local(): lax.psum_scatter(grad_term, 'dp', scatter_dimension=1, tiled=True)  58.7 us
    all_gather x1, waiting for transfers between devices, local(): weights = lax.all_gather(w_qkv, 'dp', axis=1, tiled=True)  54.3 us
    dot_general x1, matrix products, local(): jnp.dot(activ[rows:], weights, preferred_element_type=jnp.float32)  9.13 us
  transfers between devices with their start and end apart: 6, of which 4 were waited for; matrix products, arithmetic and copies ran while one was open for 4% of the time, Pallas kernels for 0%

commit v1 on v0

--- a/solution.py
+++ b/solution.py
@@ -26,7 +26,16 @@
     rows, width = frames.shape
     count = lax.axis_size("tm")
     me = lax.axis_index("tm")
-    weights = lax.all_gather(w_qkv, "dp", axis=1, tiled=True)
+    ways = lax.axis_size("dp")
+    up = [(d, (d + 1) % ways) for d in range(ways)]
+    down = [(d, (d - 1) % ways) for d in range(ways)]
+    earlier, later = ([w_qkv], [w_qkv])
+    for _ in range(ways // 2):
+        earlier.append(lax.ppermute(earlier[-1], "dp", up))
+    for _ in range((ways - 1) // 2):
+        later.append(lax.ppermute(later[-1], "dp", down))
+    line = jnp.concatenate([*earlier[::-1], *later[1:]], axis=1)
+    weights = jnp.roll(line, (lax.axis_index("dp") - ways // 2) * w_qkv.shape[1], axis=1)
     before = lax.ppermute(frames, "tm", [(i, i + 1) for i in range(count - 1)])
     far = lax.ppermute(frames[-HALF:], "tm", [(i, i + 2) for i in range(count - 2)])
     after = lax.ppermute(frames[:HALF], "tm", [(i + 1, i) for i in range(count - 1)])

time: 420 us -> 482 us (1.15)
  local copies, waits for them, and re-layouts: 13.1 us -> 47.3 us
  waiting for transfers between devices: 334 us -> 346 us
  matrix products: 32.8 us -> 40 us
  starting transfers between devices: 9.47 us -> 15.6 us
    ppermute x0 -> x7, waiting for transfers between devices: none -> 60.8 us  [the longest x4 42.5 us: local(): earlier.append(lax.ppermute(earlier[-1], 'dp', up))]
    all_gather x1 -> x0, waiting for transfers between devices: 54.3 us -> none  [local(): weights = lax.all_gather(w_qkv, 'dp', axis=1, tiled=True)]
    unnamed x13 -> x30, local copies, waits for them, and re-layouts: 5.07 us -> 34.5 us
    reduce_scatter x1, waiting for transfers between devices: 58.7 us -> 66.5 us  [local(): lax.psum_scatter(grad_term, 'dp', scatter_dimension=1, tiled=True)]
    dot_general x1, matrix products: 9.13 us -> 16.1 us  [local(): jnp.dot(activ[rows:], weights, preferred_element_type=jnp.float32)]
    unnamed x4 -> x3, waiting for transfers between devices: 215 us -> 214 us
  transfers between devices with their start and end apart: 6 -> 12, of which waited for: 4 -> 7; matrix products, arithmetic and copies ran while one was open for 4% -> 7% of each run, Pallas kernels for 0% -> 0%
where the time goes in v1:
time: 482 us; the launch traced here: 481 us
  waiting for transfers between devices  346 us (72%)
  local copies, waits for them, and re-layouts  47.3 us (10%)
  matrix products  40 us (8%)
  other arithmetic  17.1 us (4%)
  starting transfers between devices  15.6 us (3%)
  between operations  14.2 us (3%)
    unnamed x3, waiting for transfers between devices  214 us
    reduce_scatter x1, waiting for transfers between devices, local(): lax.psum_scatter(grad_term, 'dp', scatter_dimension=1, tiled=True)  66.5 us
    ppermute x4, waiting for transfers between devices, local(): earlier.append(lax.ppermute(earlier[-1], 'dp', up))  42.5 us
    unnamed x30, local copies, waits for them, and re-layouts  34.5 us
    ppermute x3, waiting for transfers between devices, local(): later.append(lax.ppermute(later[-1], 'dp', down))  18.3 us
    dot_general x1, matrix products, local(): jnp.dot(activ[rows:], weights, preferred_element_type=jnp.float32)  16.1 us
  transfers between devices with their start and end apart: 12, of which 7 were waited for; matrix products, arithmetic and copies ran while one was open for 7% of the time, Pallas kernels for 0%

profile of v1, /device:TPU:8, one launch (start us, length us, event | category | flops | bytes accessed | tf_op | source)
XLA Modules:
  0.0 480.7 jit_solution(7508311710948390545)
XLA Ops:
  7.3 22.1 %collective-permute-done.3 = bf16[1536,576]{0,1:T(8,128)(2,1)S(1)} collective-permute-done((bf16[1536,576]{0,1:T(8,128)(2,1)}, bf16[1536,576]{0,1:T(8,128)(2,1)S(1)}, u32[]{:S(2)}, u32[]{:S(2)}) %collective-permute-start.3) | collective-permute-done | bytes 1769504 | tf_op jit(solution)/shard_map/ppermute | solution.py:34
  29.4 1.7 collective-permute-start.7
  31.2 20.3 %collective-permute-done.4 = bf16[1536,576]{0,1:T(8,128)(2,1)} collective-permute-done((bf16[1536,576]{0,1:T(8,128)(2,1)S(1)}, bf16[1536,576]{0,1:T(8,128)(2,1)}, u32[]{:S(2)}, u32[]{:S(2)}) %collective-permute-start.4) | collective-permute-done | bytes 1769504 | tf_op jit(solution)/shard_map/ppermute | solution.py:34
  51.5 4.3 collective-permute-start.1
  57.8 5.2 %collective-permute-start = (bf16[2,1536]{1,0:T(2,128)(2,1)S(1)}, bf16[2,1536]{1,0:T(2,128)(2,1)S(1)}, u32[]{:S(2)}, u32[]{:S(2)}) collective-permute-start(bf16[2,1536]{1,0:T(2,128)(2,1)S(1)} %get-tuple-element.13), channel_id=1, source_target_pairs={{0,2},{1,3},{2,4},{3,5},{4,6},{5,7},{6,8},{7,9},{8,10},{9,11},{10,... | collective-permute-start | bytes 18440 | tf_op jit(solution)/shard_map/ppermute | solution.py:40
  67.2 5.2 %collective-permute-done.1 = bf16[256,1536]{1,0:T(8,128)(2,1)} collective-permute-done((bf16[256,1536]{1,0:T(8,128)(2,1)}, bf16[256,1536]{1,0:T(8,128)(2,1)}, u32[]{:S(2)}, u32[]{:S(2)}) %collective-permute-start.1) | collective-permute-done | bytes 786464 | tf_op jit(solution)/shard_map/ppermute | solution.py:39
  75.8 1.5 pad_maximum_fusion.1
  77.3 5.6 %multiply_convert_fusion = bf16[512,1536]{1,0:T(8,128)(2,1)S(1)} fusion(bf16[514,1536]{1,0:T(8,128)(2,1)S(1)} %constant_dynamic-update-slice_fusion, bf16[514,1536]{1,0:T(8,128)(2,1)S(1)} %pad_maximum_fusion.1, bf16[256,1536]{1,0:T(8,128)(2,1)S(1)} %copy-done.1, bf16[256,1536]{1,0:T(8,128)(2,1)} %collective-permute-done.1, f32[512]{0:T(512)S(1)} %get-tuple-element.16, ...), kind=kLoop, calls=%fused_computation.16 | loop fusion | flops 20447232 | bytes 9476096 | tf_op jit(solution)/shard_map/convert_element_type | solution.py:22
  82.9 12.3 %collective-permute-done.8 = bf16[1536,576]{0,1:T(8,128)(2,1)S(1)} collective-permute-done((bf16[1536,576]{0,1:T(8,128)(2,1)}, bf16[1536,576]{0,1:T(8,128)(2,1)S(1)}, u32[]{:S(2)}, u32[]{:S(2)}) %collective-permute-start.8) | collective-permute-done | bytes 1769504 | tf_op jit(solution)/shard_map/ppermute | solution.py:36
  95.2 2.1 collective-permute-start.9
  98.6 2.8 constant_dynamic-update-slice_fusion.17
  101.4 3.0 constant_dynamic-update-slice_fusion.16
  105.7 1.4 constant_dynamic-update-slice_fusion.14
  107.1 2.8 constant_dynamic-update-slice_fusion.13
  111.3 6.0 %collective-permute-done.9 = bf16[1536,576]{0,1:T(8,128)(2,1)S(1)} collective-permute-done((bf16[1536,576]{0,1:T(8,128)(2,1)S(1)}, bf16[1536,576]{0,1:T(8,128)(2,1)S(1)}, u32[]{:S(2)}, u32[]{:S(2)}) %collective-permute-start.9) | collective-permute-done | bytes 1769504 | tf_op jit(solution)/shard_map/ppermute | solution.py:36
  120.0 2.8 constant_dynamic-update-slice_fusion.9
  122.8 2.8 constant_dynamic-update-slice_fusion.8
  128.3 2.8 constant_dynamic-update-slice_fusion.5
  131.1 1.4 constant_dynamic-update-slice_fusion.4
  133.9 16.1 %fusion.5 = bf16[256,4608]{1,0:T(8,128)(2,1)} fusion(bf16[1536,9216]{0,1:T(8,128)(2,1)} %constant_dynamic-update-slice_fusion.3, s32[]{:T(128)S(6)} %select_n.25, bf16[512,1536]{1,0:T(8,128)(2,1)S(1)} %multiply_convert_fusion), kind=kOutput, calls=%fused_computation.8 | convolution fusion | flops 3625058304 | bytes 17301508 | tf_op jit(solution)/shard_map/dot_general | solution.py:46
  151.1 1.5 slice.111
  153.8 6.6 %fusion.13 = bf16[256,3072]{1,0:T(8,128)(2,1)S(1)} fusion(bf16[1536,9216]{0,1:T(8,128)(2,1)} %constant_dynamic-update-slice_fusion.3, s32[]{:T(128)S(6)} %add.53, bf16[512,1536]{1,0:T(8,128)(2,1)} %copy-done.5), kind=kOutput, calls=%fused_computation.14 | convolution fusion | flops 2416705536 | bytes 11796484 | tf_op jit(solution)/shard_map/dot_general | solution.py:47
  160.4 1.9 pad_maximum_fusion
  162.3 4.8 copy.16
  167.1 2.7 fusion.16
  169.8 6.0 %fusion.31 = (f32[16,256]{1,0:T(8,128)S(1)}, f32[16,256,512]{2,1,0:T(8,128)}) fusion(f32[16,256,512]{2,1,0:T(8,128)S(1)} %fusion.16, pred[256,512]{1,0:T(8,128)(4,1)S(1)} %compare_and_fusion), kind=kOutput, calls=%fused_computation.68 | output fusion | flops 12583423 | bytes 16924672 | tf_op jit(solution)/shard_map/sub | solution.py:61
  175.8 4.9 %fusion.17 = bf16[16,96,256]{2,1,0:T(8,128)(2,1)S(1)} fusion(f32[16,256,512]{2,1,0:T(8,128)} %get-tuple-element.20, f32[16,256]{1,0:T(8,128)S(1)} %get-tuple-element.19, bf16[512,2,16,96]{0,3,2,1:T(8,128)(2,1)S(1)} %bitcast.22), kind=kOutput, calls=%fused_computation.22 | convolution fusion | flops 407240704 | bytes 10764288 | tf_op jit(solution)/shard_map/hqk,khv->qhv/dot_general | solution.py:63
  180.7 5.1 %fusion.32 = f32[1536,1536]{0,1:T(8,128)} fusion(bf16[256,1536]{0,1:T(8,128)(2,1)S(1)} %bitcast.24, bf16[256,1536]{1,0:T(8,128)(2,1)S(1)} %copy-done), kind=kOutput, calls=%fused_computation.69 | convolution fusion | flops 1207959552 | bytes 11010048 | tf_op jit(solution)/shard_map/dot_general | solution.py:66
  185.9 66.5 %reduce-scatter.5.cloned.1.call-done = f32[1536,192]{0,1:T(8,128)} async-done(((f32[1536,1536]{0,1:T(8,128)}), f32[1536,192]{0,1:T(8,128)}) %reduce-scatter.5.cloned.1.call-update) | async-done | bytes 1179664 | tf_op jit(solution)/shard_map/reduce_scatter | solution.py:69
  252.4 2.9 copy.19
  255.3 4.6 convolution_convert_fusion
  259.9 213.9 %reduce-scatter.7.cloned.1.call-done = f32[48,192]{1,0:T(8,128)} async-done(((f32[1536,192]{1,0:T(8,128)}), f32[48,192]{1,0:T(8,128)}) %reduce-scatter.7.cloned.1.call-update) | async-done | bytes 36880
  (49 shorter events, 22.7 us)
Async XLA Ops:
  7.2 173.5 %copy-start = (bf16[256,1536]{1,0:T(8,128)(2,1)S(1)}, bf16[256,1536]{1,0:T(8,128)(2,1)}, u32[]{:S(2)}) copy-start(bf16[256,1536]{1,0:T(8,128)(2,1)} %param.13) | copy-start | bytes 2359300
  7.2 68.6 %copy-start.1 = (bf16[256,1536]{1,0:T(8,128)(2,1)S(1)}, bf16[256,1536]{1,0:T(8,128)(2,1)}, u32[]{:S(2)}) copy-start(bf16[256,1536]{1,0:T(8,128)(2,1)} %param.7) | copy-start | bytes 2359300
  7.2 245.2 %reduce-scatter.5.cloned.1.call-start = ((), (), s32[]{:S(2)}) async-start(), calls=%async_computation.2 | async-start | bytes 10616832 | tf_op jit(solution)/shard_map/reduce_scatter | solution.py:69
  7.2 22.2 %collective-permute-start.3 = (bf16[1536,576]{0,1:T(8,128)(2,1)}, bf16[1536,576]{0,1:T(8,128)(2,1)S(1)}, u32[]{:S(2)}, u32[]{:S(2)}) collective-permute-start(bf16[1536,576]{0,1:T(8,128)(2,1)} %param.11), channel_id=1, source_target_pairs={{0,32},{32,64},{64,96},{96,128},{128,160},{160,192},{192,224},{224... | collective-permute-start | bytes 5308424 | tf_op jit(solution)/shard_map/ppermute | solution.py:34
  29.4 22.1 %collective-permute-start.4 = (bf16[1536,576]{0,1:T(8,128)(2,1)S(1)}, bf16[1536,576]{0,1:T(8,128)(2,1)}, u32[]{:S(2)}, u32[]{:S(2)}) collective-permute-start(bf16[1536,576]{0,1:T(8,128)(2,1)S(1)} %collective-permute-done.3), channel_id=1, source_target_pairs={{0,32},{32,64},{64,96},{96,128},{128,160},{160,192},{192,224},{224... | collective-permute-start | bytes 5308424 | tf_op jit(solution)/shard_map/ppermute | solution.py:34
  29.4 45.4 %collective-permute-start.7 = (bf16[1536,576]{0,1:T(8,128)(2,1)}, bf16[1536,576]{0,1:T(8,128)(2,1)}, u32[]{:S(2)}, u32[]{:S(2)}) collective-permute-start(bf16[1536,576]{0,1:T(8,128)(2,1)} %param.11), channel_id=1, source_target_pairs={{0,224},{32,0},{64,32},{96,64},{128,96},{160,128},{192,160},{224,1... | collective-permute-start | bytes 5308424 | tf_op jit(solution)/shard_map/ppermute | solution.py:36
  51.5 23.4 %collective-permute-start.5 = (bf16[1536,576]{0,1:T(8,128)(2,1)}, bf16[1536,576]{0,1:T(8,128)(2,1)}, u32[]{:S(2)}, u32[]{:S(2)}) collective-permute-start(bf16[1536,576]{0,1:T(8,128)(2,1)} %collective-permute-done.4), channel_id=1, source_target_pairs={{0,32},{32,64},{64,96},{96,128},{128,160},{160,192},{192,224},{224... | collective-permute-start | bytes 5308424 | tf_op jit(solution)/shard_map/ppermute | solution.py:34
  51.5 21.0 %collective-permute-start.1 = (bf16[256,1536]{1,0:T(8,128)(2,1)}, bf16[256,1536]{1,0:T(8,128)(2,1)}, u32[]{:S(2)}, u32[]{:S(2)}) collective-permute-start(bf16[256,1536]{1,0:T(8,128)(2,1)} %param.7), channel_id=1, source_target_pairs={{0,1},{1,2},{2,3},{3,4},{4,5},{5,6},{6,7},{7,8},{8,9},{9,10},{10,1... | collective-permute-start | bytes 2359304 | tf_op jit(solution)/shard_map/ppermute | solution.py:39
  56.5 19.2 %collective-permute-start.2 = (bf16[2,1536]{1,0:T(2,128)(2,1)S(1)}, bf16[2,1536]{1,0:T(2,128)(2,1)S(1)}, u32[]{:S(2)}, u32[]{:S(2)}) collective-permute-start(bf16[2,1536]{1,0:T(2,128)(2,1)S(1)} %get-tuple-element.14), channel_id=1, source_target_pairs={{1,0},{2,1},{3,2},{4,3},{5,4},{6,5},{7,6},{8,7},{9,8},{10,9},{11,1... | collective-permute-start | bytes 18440 | tf_op jit(solution)/shard_map/ppermute | solution.py:41
  57.8 17.9 %collective-permute-start = (bf16[2,1536]{1,0:T(2,128)(2,1)S(1)}, bf16[2,1536]{1,0:T(2,128)(2,1)S(1)}, u32[]{:S(2)}, u32[]{:S(2)}) collective-permute-start(bf16[2,1536]{1,0:T(2,128)(2,1)S(1)} %get-tuple-element.13), channel_id=1, source_target_pairs={{0,2},{1,3},{2,4},{3,5},{4,6},{5,7},{6,8},{7,9},{8,10},{9,11},{10,... | collective-permute-start | bytes 18440 | tf_op jit(solution)/shard_map/ppermute | solution.py:40
  74.8 20.4 %collective-permute-start.8 = (bf16[1536,576]{0,1:T(8,128)(2,1)}, bf16[1536,576]{0,1:T(8,128)(2,1)S(1)}, u32[]{:S(2)}, u32[]{:S(2)}) collective-permute-start(bf16[1536,576]{0,1:T(8,128)(2,1)} %collective-permute-done.7), channel_id=1, source_target_pairs={{0,224},{32,0},{64,32},{96,64},{128,96},{160,128},{192,160},{224,1... | collective-permute-start | bytes 5308424 | tf_op jit(solution)/shard_map/ppermute | solution.py:36
  74.8 22.4 %collective-permute-start.6 = (bf16[1536,576]{0,1:T(8,128)(2,1)}, bf16[1536,576]{0,1:T(8,128)(2,1)S(1)}, u32[]{:S(2)}, u32[]{:S(2)}) collective-permute-start(bf16[1536,576]{0,1:T(8,128)(2,1)} %collective-permute-done.5), channel_id=1, source_target_pairs={{0,32},{32,64},{64,96},{96,128},{128,160},{160,192},{192,224},{224... | collective-permute-start | bytes 5308424 | tf_op jit(solution)/shard_map/ppermute | solution.py:34
  82.9 51.0 %copy-start.5 = (bf16[512,1536]{1,0:T(8,128)(2,1)}, bf16[512,1536]{1,0:T(8,128)(2,1)S(1)}, u32[]{:S(2)}) copy-start(bf16[512,1536]{1,0:T(8,128)(2,1)S(1)} %multiply_convert_fusion) | copy-start | bytes 4718596
  95.2 22.1 %collective-permute-start.9 = (bf16[1536,576]{0,1:T(8,128)(2,1)S(1)}, bf16[1536,576]{0,1:T(8,128)(2,1)S(1)}, u32[]{:S(2)}, u32[]{:S(2)}) collective-permute-start(bf16[1536,576]{0,1:T(8,128)(2,1)S(1)} %collective-permute-done.8), channel_id=1, source_target_pairs={{0,224},{32,0},{64,32},{96,64},{128,96},{160,128},{192,160},{224,1... | collective-permute-start | bytes 5308424 | tf_op jit(solution)/shard_map/ppermute | solution.py:36
  101.4 4.3 copy-start.2
  162.3 4.8 copy-start.4
  169.8 6.0 %copy-start.3 = (bf16[512,3072]{0,1:T(8,128)(2,1)S(1)}, bf16[512,3072]{0,1:T(8,128)(2,1)}, u32[]{:S(2)}) copy-start(bf16[512,3072]{0,1:T(8,128)(2,1)} %copy.16) | copy-start | bytes 9437188
  185.8 288.1 %reduce-scatter.7.cloned.1.call-start = ((), (), s32[]{:S(2)}) async-start(), calls=%async_computation.3 | async-start | bytes 1622016
Sparse Core Ops, SparseCore 0:
  185.9 66.4 reduce-scatter.4
  256.8 217.0 reduce-scatter.6
